TPU v7x, 128 devices: a whole 4x4x4 slice. The times are simulated.
128 devices in a mesh: wide: 16 (over y, z), grp: 8 (over x, core).
Axes of the slice: x: 4, y: 4, z: 4, core: 2. Of those that a mesh axis runs over, the one named last changes fastest.
Arguments:
- eta_hat: bfloat16 [2, 2048, 2048], P(None, ('wide', 'grp')), may hold values from -0.0008544922 to 0.0008544922
- phi_hat: bfloat16 [2, 2048, 2048], P(None, ('wide', 'grp')), may hold values from -0.00061035156 to 0.00061035156
- patch_tiles: int32 [256], replicated, may hold values from 0 to 1023, as said below
- fraction: bfloat16 [2, 128, 64, 128, 128], P(None, ('wide', 'grp')), may hold values from 0 to 1
Outputs:
- surface: float32 [2048, 2048], P(('wide', 'grp'))
- fraction_next: bfloat16 [2, 128, 64, 128, 128], P(None, ('wide', 'grp'))
- tendency: float32 [2, 2048, 2048], P(None, ('wide', 'grp'))
Inputs may be any that keep to these rules, and one draw needn't show every extreme that they name: `patch_tiles`: for each g below 8, entries g * 32 to (g + 1) * 32 - 1 are distinct tiles, in ascending order, whose column t % 32 lies in [g * 4, (g + 1) * 4). Of these, the tiles of one band (rows (t // 32) // 2 equal) are at most 8, and in every group one band holds exactly 8.
All inputs are finite; a program needn't handle non-finite values.
Results may differ from a plain program's by a relative error of at most 0.019.
Values may be sent and summed in bfloat16 or wider, within the bound.
A program may use at most 192 MiB of HBM per device.

v0:
```python
import math
import jax
import jax.numpy as jnp
from jax import lax
from jax.sharding import PartitionSpec as P

RADIX = 32
TS = 64
Z_BOTTOM = -2.0
Z_TOP = 2.0
DECAY_RATE = 0.5
COURANT = 0.3


def for_sending(shard):

    def short(part):
        return part.astype(jnp.bfloat16) if part.dtype == jnp.float32 else part

    return jax.tree.map(short, shard)


def refine(field):
    return jnp.repeat(jnp.repeat(field, 2, axis=0), 2, axis=1)


def upwind_flux(values, speeds, axis):
    widths = tuple(((1, 1) if dim_index == axis else (0, 0) for dim_index in range(3)))
    padded = jnp.pad(values, widths, mode="edge")
    speed_pad = jnp.pad(speeds, widths, mode="edge")
    count_faces = padded.shape[axis] - 1
    left_vals = lax.slice_in_dim(padded, 0, count_faces, axis=axis)
    right_vals = lax.slice_in_dim(padded, 1, count_faces + 1, axis=axis)
    face_speed = 0.5 * (
        lax.slice_in_dim(speed_pad, 0, count_faces, axis=axis)
        + lax.slice_in_dim(speed_pad, 1, count_faces + 1, axis=axis)
    )
    face_flux = jnp.maximum(face_speed, 0.0) * left_vals + jnp.minimum(face_speed, 0.0) * right_vals
    return lax.slice_in_dim(face_flux, 1, count_faces, axis=axis) - lax.slice_in_dim(
        face_flux, 0, count_faces - 1, axis=axis
    )


def patch_step(state, height, along_x, along_y):
    levels = state.shape[0]
    side = state.shape[1]
    spacing = (Z_TOP - Z_BOTTOM) / levels
    level_z = (Z_BOTTOM + (jnp.arange(levels, dtype=jnp.float32) + 0.5) * spacing)[:, None, None]
    fine_h = refine(height)[None]
    from_sea = jnp.clip((fine_h - level_z) / spacing + 0.5, 0.0, 1.0)
    position = jnp.arange(side, dtype=jnp.float32)
    edge_dist = jnp.minimum(position, side - 1.0 - position)
    distance = jnp.minimum(edge_dist[:, None], edge_dist[None, :])
    weight = 0.3 + 0.7 * jnp.exp(-8.0 * distance / side)
    blended = weight * from_sea + (1.0 - weight) * state.astype(jnp.float32)
    profile = jnp.exp(DECAY_RATE * (level_z - Z_TOP))
    speed_x = refine(along_x)[None] * profile
    speed_y = refine(along_y)[None] * profile
    moved = blended - COURANT * (
        upwind_flux(blended, speed_x, 2) + upwind_flux(blended, speed_y, 1)
    )
    updated = jnp.clip(moved, 0.0, 1.0)
    column = Z_BOTTOM + spacing * jnp.sum(updated, axis=0)
    coarse = column.reshape(side // 2, 2, side // 2, 2).mean(axis=(1, 3))
    return (updated.astype(jnp.bfloat16), coarse)


def small_tables(length):
    index_row = jnp.arange(length, dtype=jnp.int32)
    phase = index_row[:, None] * index_row[None, :] % length
    angle = phase.astype(jnp.float32) * (2.0 * math.pi / length)
    return (jnp.cos(angle).astype(jnp.bfloat16), jnp.sin(angle).astype(jnp.bfloat16))


def contract(data, table, pattern):
    return jnp.einsum(pattern, data, table, preferred_element_type=jnp.float32)


def factored_transform(real_in, imag_in, direction_sign, real_only):
    length = real_in.shape[-1]
    leading = real_in.shape[:-1]
    inner_size = length // RADIX
    cos_p, sin_p = small_tables(RADIX)
    cos_q, sin_q = small_tables(inner_size)
    split_re = real_in.reshape(leading + (RADIX, inner_size))
    segment_re = contract(split_re, cos_p, "...pq,pk->...kq")
    segment_im = direction_sign * contract(split_re, sin_p, "...pq,pk->...kq")
    if imag_in is not None:
        split_im = imag_in.reshape(leading + (RADIX, inner_size))
        segment_re = segment_re - direction_sign * contract(split_im, sin_p, "...pq,pk->...kq")
        segment_im = segment_im + contract(split_im, cos_p, "...pq,pk->...kq")
    first_idx = jnp.arange(RADIX, dtype=jnp.int32)[:, None]
    second_idx = jnp.arange(inner_size, dtype=jnp.int32)[None, :]
    angle = (first_idx * second_idx % length).astype(jnp.float32) * (2.0 * math.pi / length)
    twist_cos = jnp.cos(angle)
    twist_sin = jnp.sin(angle)
    turned_re = (segment_re * twist_cos - direction_sign * segment_im * twist_sin).astype(
        jnp.bfloat16
    )
    turned_im = (segment_im * twist_cos + direction_sign * segment_re * twist_sin).astype(
        jnp.bfloat16
    )
    out_re = contract(turned_re, cos_q, "...kq,qm->...km") - direction_sign * contract(
        turned_im, sin_q, "...kq,qm->...km"
    )
    out_re = jnp.swapaxes(out_re, -1, -2).reshape(leading + (length,))
    if real_only:
        return out_re
    out_im = contract(turned_im, cos_q, "...kq,qm->...km") + direction_sign * contract(
        turned_re, sin_q, "...kq,qm->...km"
    )
    out_im = jnp.swapaxes(out_im, -1, -2).reshape(leading + (length,))
    return (out_re, out_im)


def signed_waves(index_values, length):
    signed = (index_values + length // 2) % length - length // 2
    return signed.astype(jnp.float32) * (2.0 * math.pi / length)


def shards(eta_hat, phi_hat, patch_tiles, fraction):
    row_count = eta_hat.shape[1]
    length = eta_hat.shape[2]
    n_wide = lax.axis_size("wide")
    me_wide = lax.axis_index("wide")
    me_grp = lax.axis_index("grp")
    me_flat = lax.axis_index(("wide", "grp"))
    wave_cols = signed_waves(jnp.arange(length, dtype=jnp.int32), length)
    wave_rows = signed_waves(me_flat * row_count + jnp.arange(row_count, dtype=jnp.int32), length)
    phi_re = phi_hat[0].astype(jnp.float32)
    phi_im = phi_hat[1].astype(jnp.float32)
    real_in = jnp.stack(
        [
            eta_hat[0],
            (-wave_rows[:, None] * phi_im).astype(jnp.bfloat16),
            (-wave_cols[None, :] * phi_im).astype(jnp.bfloat16),
        ]
    )
    imag_in = jnp.stack(
        [
            eta_hat[1],
            (wave_rows[:, None] * phi_re).astype(jnp.bfloat16),
            (wave_cols[None, :] * phi_re).astype(jnp.bfloat16),
        ]
    )
    half_re, half_im = factored_transform(real_in, imag_in, 1.0, False)
    inverse_rows = jnp.swapaxes(
        jnp.concatenate([half_re.astype(jnp.bfloat16), half_im.astype(jnp.bfloat16)]), 1, 2
    )
    turned = lax.all_to_all(inverse_rows, ("wide", "grp"), split_axis=1, concat_axis=2, tiled=True)
    physical = factored_transform(turned[0:3], turned[3:6], 1.0, True)
    band_fields = lax.all_to_all(
        physical.astype(jnp.bfloat16), "grp", split_axis=2, concat_axis=1, tiled=True
    ).astype(physical.dtype)
    band_rows = band_fields.shape[1]
    band_cols = band_fields.shape[2]
    tile_rows = band_rows // TS
    tile_cols = band_cols // TS
    tiles_side = length // TS
    per_group = 2 * n_wide
    group_list = lax.dynamic_slice_in_dim(patch_tiles, me_grp * per_group, per_group)
    row_of = group_list // tiles_side
    col_of = group_list % tiles_side - me_grp * tile_cols
    my_ranks = jnp.arange(2, dtype=jnp.int32) * n_wide + me_wide
    local_t = jnp.arange(tile_rows * tile_cols, dtype=jnp.int32)
    tile_id = (
        (me_wide * tile_rows + local_t // tile_cols) * tiles_side
        + me_grp * tile_cols
        + local_t % tile_cols
    )
    matches = tile_id[:, None] == group_list[None, :]
    active = jnp.any(matches, axis=1)
    rank_index = jnp.sum(
        jnp.where(matches, jnp.arange(per_group, dtype=jnp.int32)[None, :], 0), axis=1
    )
    column_strip = lax.all_gather(
        band_fields.astype(jnp.bfloat16), "wide", axis=1, tiled=True
    ).astype(band_fields.dtype)

    def pick_strip(rank):
        return lax.dynamic_slice(
            column_strip, (0, row_of[rank] * TS, col_of[rank] * TS), (3, TS, TS)
        )

    footprints = jax.vmap(pick_strip)(my_ranks)
    new_states, coarse = jax.vmap(patch_step)(
        fraction[:, 0], footprints[:, 0], footprints[:, 1], footprints[:, 2]
    )
    coarse_flat = coarse.reshape(2, TS * TS)
    every_result = (
        lax.all_gather(
            coarse_flat.reshape(2, 1, TS * TS).astype(jnp.bfloat16), "wide", axis=1, tiled=True
        )
        .astype(jnp.float32)
        .reshape(per_group, TS * TS)
    )
    picked = every_result[rank_index]
    band_tiles = (
        band_fields[0]
        .reshape(tile_rows, TS, tile_cols, TS)
        .transpose(0, 2, 1, 3)
        .reshape(tile_rows * tile_cols, TS * TS)
    )
    corrected = jnp.where(active[:, None], picked, band_tiles)
    surface_band = (
        corrected.reshape(tile_rows, tile_cols, TS, TS)
        .transpose(0, 2, 1, 3)
        .reshape(band_rows, band_cols)
    )
    surface = lax.all_to_all(
        for_sending(surface_band), "grp", split_axis=0, concat_axis=1, tiled=True
    ).astype(surface_band.dtype)
    along_x = physical[1]
    along_y = physical[2]
    drive = (-(surface + 0.5 * (along_x * along_x + along_y * along_y))).astype(jnp.bfloat16)
    drive_re, drive_im = factored_transform(drive, None, -1.0, False)
    pair_rows = jnp.swapaxes(
        jnp.stack([drive_re.astype(jnp.bfloat16), drive_im.astype(jnp.bfloat16)]), 1, 2
    )
    pair_cols = lax.all_to_all(pair_rows, ("wide", "grp"), split_axis=1, concat_axis=2, tiled=True)
    spec_re, spec_im = factored_transform(pair_cols[0], pair_cols[1], -1.0, False)
    tendency = jnp.stack([spec_re, spec_im]) * (1.0 / length)
    return (surface, new_states[:, None], tendency)


def solution(mesh):
    placed = (
        P(None, ("wide", "grp"), None),
        P(None, ("wide", "grp"), None),
        P(),
        P(None, ("wide", "grp"), None, None, None),
    )
    return jax.shard_map(
        shards,
        mesh=mesh,
        in_specs=placed,
        out_specs=(
            P(("wide", "grp"), None),
            P(None, ("wide", "grp"), None, None, None),
            P(None, ("wide", "grp"), None),
        ),
        check_vma=False,
    )
```

profile of v0, /device:TPU:1, one launch (start us, length us, event | category | flops | bytes accessed | tf_op | source)
XLA Modules:
  0.0 338.8 jit_solution(14497222716978649175)
XLA Ops:
  15.9 4.1 %copy.124 = bf16[6,2048,16]{2,0,1:T(8,128)(2,1)} copy(bf16[6,2048,16]{1,2,0:T(8,128)(2,1)S(1)} %maximum_bitcast_fusion) | data formatting | bytes 786432 | tf_op jit(solution)/shard_map/transpose | solution.py:147
  20.0 5.6 %reshape.527 = bf16[128,2,768]{2,1,0:T(2,128)(2,1)S(1)} reshape(bf16[2048,6,16]{2,1,0:T(8,128)(2,1)} %bitcast.240) | data formatting | bytes 786432
  25.6 24.1 %all_to_all.58 = bf16[128,2,768]{2,1,0:T(2,128)(2,1)S(1)} all-to-all(bf16[128,2,768]{2,1,0:T(2,128)(2,1)S(1)} %reshape.527), channel_id=1, replica_groups=mesh['wide'=16,'grp'=8] {'wide','grp'}, dimensions={0} | all-to-all | bytes 786432 | tf_op jit(solution)/shard_map/all_to_all | solution.py:150
  49.7 4.8 %reshape.528 = bf16[2048,6,16]{2,1,0:T(8,128)(2,1)} reshape(bf16[128,2,768]{2,1,0:T(2,128)(2,1)S(1)} %all_to_all.58) | data formatting | bytes 786432
  54.6 6.1 %copy.158 = bf16[6,128,16,16]{2,1,3,0:T(8,128)(2,1)S(1)} copy(bf16[6,128,16,16]{3,0,2,1:T(8,128)(2,1)} %bitcast.239) | data formatting | bytes 786432 | tf_op jit(solution)/shard_map/all_to_all | solution.py:150
  62.6 4.3 %copy.126 = bf16[3,16,128,16]{3,2,1,0:T(8,128)(2,1)S(1)} copy(bf16[3,16,128,16]{1,2,3,0:T(8,128)(2,1)} %get-tuple-element.58) | data formatting | bytes 393216 | tf_op jit(solution)/shard_map/slice | solution.py:151
  70.2 3.1 copy.127
  77.9 3.4 %copy.159 = bf16[3,16,64,32]{1,0,3,2:T(4,128)(2,1)S(1)} copy(bf16[3,16,64,32]{2,3,1,0:T(8,128)(2,1)S(1)} %get-tuple-element.82) | data formatting | bytes 393216 | tf_op jit(solution)/shard_map/convert_element_type | solution.py:153
  83.2 9.3 %all_to_all.59 = bf16[8,2,6144]{2,1,0:T(2,128)(2,1)S(1)} all-to-all(bf16[8,2,6144]{2,1,0:T(2,128)(2,1)S(1)} %reshape.529), channel_id=1, replica_groups=mesh['wide'=16,'grp'=8] {'grp'}, dimensions={0} | all-to-all | bytes 393216 | tf_op jit(solution)/shard_map/all_to_all | solution.py:152
  94.5 2.0 copy.161
  101.1 39.6 %all-gather.2.cloned.1.call-done = bf16[3,2048,256]{2,1,0:T(8,128)(2,1)} async-done(((bf16[3,128,256]{2,1,0:T(8,128)(2,1)}), bf16[3,2048,256]{2,1,0:T(8,128)(2,1)}) %all-gather.2.cloned.1.call-update) | async-done | bytes 3145744 | tf_op jit(solution)/shard_map/all_gather | solution.py:176
  140.7 5.1 %convert_element_type.418 = f32[3,2048,256]{2,1,0:T(8,128)} convert(bf16[3,2048,256]{2,1,0:T(8,128)(2,1)} %all-gather.2.cloned.1.call-done) | non-fusion elementwise | flops 1572864 | bytes 9437184 | tf_op jit(solution)/shard_map/convert_element_type | solution.py:178
  145.8 5.9 %while.1 = (s32[]{:T(128)}, f32[3,2048,256]{2,1,0:T(8,128)}, s32[2,3]{1,0:T(2,128)S(1)}, f32[2,3,64,64]{3,2,1,0:T(8,128)S(1)}, s32[]{:T(128)}) while((s32[]{:T(128)}, f32[3,2048,256]{2,1,0:T(8,128)}, s32[2,3]{1,0:T(2,128)S(1)}, f32[2,3,64,64]{3,2,1,0:T(8,128)S(1)}, s32[]{:T(128)}) %tuple.55), condition=%wide.while_cond, body=%wide.while_body.sunk | while | flops 2 | bytes 147581 | solution.py:181
  146.4 2.3 bitcast_dynamic-update-slice_fusion.2
  149.3 2.3 bitcast_dynamic-update-slice_fusion.2
  153.6 3.9 %fusion.8 = f32[2,64,128,128]{3,2,1,0:T(8,128)S(1)} fusion(bf16[2,1,64,128,128]{4,3,2,1,0:T(8,128)(2,1)} %param.7, f32[128,128]{1,0:T(8,128)S(1)} %get-tuple-element.81, f32[64]{0:T(128)S(1)} %fusion.129, f32[2,128,128]{2,1,0:T(8,128)S(1)} %copy.134, f32[128,128]{1,0:T(8,128)S(1)} %get-tuple-element.80), kind=kLoop, calls=%fused_computation.22 | loop fusion | flops 16777216 | bytes 12845312 | tf_op jit(solution)/shard_map/vmap()/add | solution.py:55
  157.6 7.7 %fusion.246 = (f32[2,64,128,1]{3,2,1,0:T(8,128)}, f32[2,64,128,1]{3,2,1,0:T(8,128)}) fusion(f32[2,64,128,128]{3,2,1,0:T(8,128)S(1)} %fusion.8), kind=kLoop, calls=%fused_computation.353 | loop fusion | bytes 262144 | tf_op jit(solution)/shard_map/vmap(jit(_pad))/slice | solution.py:29
  166.5 5.4 %broadcast_multiply_fusion.1 = (f32[2,64,128,128]{3,2,1,0:T(8,128)}, f32[2,64,128,128]{3,2,1,0:T(8,128)S(1)}) fusion(f32[64]{0:T(128)S(1)} %multiply_exponential_fusion, f32[2,128,128]{2,1,0:T(8,128)S(1)} %copy.137, f32[2,128,128]{2,1,0:T(8,128)S(1)} %copy.139), kind=kLoop, calls=%fused_computation.25 | loop fusion | flops 4194304 | bytes 17039616 | tf_op jit(solution)/shard_map/vmap()/mul | solution.py:57
  171.9 3.2 copy-done.1
  175.2 13.3 %fusion.245 = (f32[2,64,128,1]{3,2,1,0:T(8,128)}, f32[2,64,128,1]{3,2,1,0:T(8,128)}) fusion(f32[2,64,128,128]{3,2,1,0:T(8,128)} %get-tuple-element.78), kind=kLoop, calls=%fused_computation.352 | loop fusion | bytes 262144 | tf_op jit(solution)/shard_map/vmap(jit(_pad))/slice | solution.py:30
  188.5 12.6 %fusion.3 = f32[2,64,129,128]{3,2,1,0:T(8,128)} fusion(f32[2,64,128,128]{3,2,1,0:T(8,128)S(1)} %bitcast.236, f32[2,64,1,128]{3,2,1,0:T(1,128)S(1)} %get-tuple-element.56, f32[2,64,1,128]{3,2,1,0:T(1,128)S(1)} %get-tuple-element.55, f32[2,64,1,128]{3,2,1,0:T(1,128)S(1)} %get-tuple-element.54, f32[2,64,128,128]{3,2,1,0:T(8,128)} %copy-done.1, ...), kind=kLoop, calls=%fused_computation.13 | loop fusion | flops 23248896 | bytes 25493504 | tf_op jit(solution)/shard_map/vmap()/add | solution.py:38
  201.1 25.7 %fusion.1 = f32[2,64,128,129]{3,2,1,0:T(8,128)} fusion(f32[2,64,128,128]{3,2,1,0:T(8,128)S(1)} %bitcast.236, f32[2,64,128,1]{3,2,1,0:T(8,128)} %get-tuple-element.52, f32[2,64,128,1]{3,2,1,0:T(8,128)} %get-tuple-element.51, f32[2,64,128,1]{3,2,1,0:T(8,128)} %get-tuple-element.50, f32[2,64,128,128]{3,2,1,0:T(8,128)} %get-tuple-element.78, ...), kind=kLoop, calls=%fused_computation.8 | loop fusion | flops 23248896 | bytes 25493504 | tf_op jit(solution)/shard_map/vmap()/add | solution.py:38
  226.8 22.0 %convert_bitcast_fusion = (bf16[2,1,64,128,128]{4,3,2,1,0:T(8,128)(2,1)}, f32[2,64,128,128]{3,2,1,0:T(8,128)}) fusion(f32[2,64,129,128]{3,2,1,0:T(8,128)} %fusion.3, f32[2,64,128,129]{3,2,1,0:T(8,128)} %fusion.1, bf16[2,1,64,128,128]{4,3,2,1,0:T(8,128)(2,1)} %param.7, f32[128,128]{1,0:T(8,128)S(1)} %get-tuple-element.81, f32[64]{0:T(128)S(1)} %fusion.129, ...), kind=kLoop, calls=%fused_computation.23 | loop fusion | flops 31457280 | bytes 50594048 | tf_op jit(solution)/shard_map/broadcast_in_dim | solution.py:223
  248.9 3.8 %reduce_sum.29 = f32[2,128,128]{2,1,0:T(8,128)S(1)} reduce(f32[2,64,128,128]{3,2,1,0:T(8,128)} %get-tuple-element.44, f32[]{:T(128)} %constant.200.clone.1), dimensions={1}, to_apply=%region_1.2 | reduce | flops 2064384 | bytes 8519684 | tf_op jit(solution)/shard_map/vmap()/reduce_sum | solution.py:63
  252.7 9.8 %add.508 = f32[2,64,2,64,2]{4,3,2,1,0:T(8,128)} reshape(f32[2,128,128]{2,1,0:T(8,128)S(1)} %multiply_add_fusion) | data formatting | bytes 262144 | tf_op jit(solution)/shard_map/vmap()/add | solution.py:63
  262.5 4.5 %reduce_sum.30 = f32[2,64,64]{2,1,0:T(8,128)S(1)} reduce(f32[2,64,2,64,2]{4,3,2,1,0:T(8,128)} %add.508, f32[]{:T(128)} %constant.200.clone.1), dimensions={2,4}, to_apply=%region_2.3 | reduce | flops 24576 | bytes 163844 | tf_op jit(solution)/shard_map/vmap()/reduce_sum | solution.py:64
  267.2 17.1 %all_gather.7 = bf16[2,16,4096]{2,0,1:T(2,128)(2,1)S(1)} all-gather(bf16[2,1,4096]{2,0,1:T(2,128)(2,1)S(1)} %convert_element_type.422), channel_id=1, replica_groups=mesh['wide'=16,'grp'=8] {'wide'}, dimensions={1}, use_global_device_ids=true | all-gather | bytes 278528 | tf_op jit(solution)/shard_map/all_gather | solution.py:191
  286.1 11.0 %all-to-all-start.2 = ((bf16[8,16,256]{2,1,0:T(8,128)(2,1)}), bf16[8,16,256]{2,1,0:T(8,128)(2,1)S(1)}, u32[]{:S(2)}, u32[]{:S(2)}) async-start(bf16[8,16,256]{2,1,0:T(8,128)(2,1)} %convert_element_type.425), calls=%async_computation.2 | async-start | bytes 131072 | tf_op jit(solution)/shard_map/all_to_all | solution.py:210
  297.5 4.4 %all-to-all-done.2 = bf16[8,16,256]{2,1,0:T(8,128)(2,1)S(1)} async-done(((bf16[8,16,256]{2,1,0:T(8,128)(2,1)}), bf16[8,16,256]{2,1,0:T(8,128)(2,1)S(1)}, u32[]{:S(2)}, u32[]{:S(2)}) %all-to-all-start.2) | async-done | bytes 65568 | tf_op jit(solution)/shard_map/all_to_all | solution.py:210
  307.2 4.9 %all-to-all-start.3 = ((bf16[128,2,256]{2,1,0:T(2,128)(2,1)}), bf16[128,2,256]{2,1,0:T(2,128)(2,1)S(1)}, u32[]{:S(2)}, u32[]{:S(2)}) async-start(bf16[128,2,256]{2,1,0:T(2,128)(2,1)} %reshape.531), calls=%async_computation.3 | async-start | bytes 262144 | tf_op jit(solution)/shard_map/all_to_all | solution.py:220
  312.8 9.3 %all-to-all-done.3 = bf16[128,2,256]{2,1,0:T(2,128)(2,1)S(1)} async-done(((bf16[128,2,256]{2,1,0:T(2,128)(2,1)}), bf16[128,2,256]{2,1,0:T(2,128)(2,1)S(1)}, u32[]{:S(2)}, u32[]{:S(2)}) %all-to-all-start.3) | async-done | bytes 131104 | tf_op jit(solution)/shard_map/all_to_all | solution.py:220
  322.7 2.0 copy.162
  (158 shorter events, 46.4 us)
Async XLA Ops:
  7.2 133.5 %all-gather.2.cloned.1.call-start = ((), (), s32[]{:S(2)}) async-start(), calls=%async_computation.4 | async-start | bytes 3342336 | tf_op jit(solution)/shard_map/all_gather | solution.py:176
  7.3 6.5 %copy-start.3 = (f32[32,64]{1,0:T(8,128)}, f32[32,64]{1,0:T(8,128)S(1)}, u32[]{:S(2)}) copy-start(f32[32,64]{1,0:T(8,128)S(1)} %get-tuple-element.88) | copy-start | bytes 24580
  62.6 7.6 %copy-start.2 = (bf16[3,16,128,16]{1,2,3,0:T(8,128)(2,1)S(1)}, bf16[3,16,128,16]{1,2,3,0:T(8,128)(2,1)}, u32[]{:S(2)}) copy-start(bf16[3,16,128,16]{1,2,3,0:T(8,128)(2,1)} %get-tuple-element.57) | copy-start | bytes 589828
  70.2 6.9 %copy-start.4 = (f32[32,64]{1,0:T(8,128)S(1)}, f32[32,64]{1,0:T(8,128)}, u32[]{:S(2)}) copy-start(f32[32,64]{1,0:T(8,128)} %copy-done.3) | copy-start | bytes 24580
  77.1 19.5 %copy-start.8 = (s32[256]{0:T(256)S(1)}, s32[256]{0:T(256)}, u32[]{:S(2)}) copy-start(s32[256]{0:T(256)} %param.6) | copy-start | bytes 3076
  151.7 0.7 copy-start.5
  157.5 8.4 %copy-start = (f32[2,64,128,128]{3,2,1,0:T(8,128)}, f32[2,64,128,128]{3,2,1,0:T(8,128)S(1)}, u32[]{:S(2)}) copy-start(f32[2,64,128,128]{3,2,1,0:T(8,128)S(1)} %fusion.8) | copy-start | bytes 25165828
  166.4 22.1 %slice-start = ((s8[8388608]{0:T(1024)(128)(4,1)}), s8[4194304]{0:T(1024)(128)(4,1)S(1)}, s32[]{:S(2)}) async-start(s8[8388608]{0:T(1024)(128)(4,1)} %bitcast.235), calls=%async_computation.5 | async-start | bytes 8388608
  171.9 3.2 copy-start.1
  175.2 13.3 %slice-start.1 = ((s8[8388608]{0:T(1024)(128)(4,1)}), s8[4194304]{0:T(1024)(128)(4,1)S(1)}, s32[]{:S(2)}) async-start(s8[8388608]{0:T(1024)(128)(4,1)} %bitcast.235), calls=%async_computation.6 | async-start | bytes 8388608
  252.7 32.5 %copy-start.7 = (pred[2,4]{1,0:T(4,128)(4,1)S(1)}, pred[2,4]{1,0:T(4,128)(4,1)}, u32[]{:S(2)}) copy-start(pred[2,4]{1,0:T(4,128)(4,1)} %broadcast_in_dim.29) | copy-start | bytes 28
  262.5 39.9 %copy-start.6 = (f32[32,64]{1,0:T(8,128)S(1)}, f32[32,64]{1,0:T(8,128)}, u32[]{:S(2)}) copy-start(f32[32,64]{1,0:T(8,128)} %get-tuple-element.93) | copy-start | bytes 24580
  286.1 15.8 %all-to-all-start.2 = ((bf16[8,16,256]{2,1,0:T(8,128)(2,1)}), bf16[8,16,256]{2,1,0:T(8,128)(2,1)S(1)}, u32[]{:S(2)}, u32[]{:S(2)}) async-start(bf16[8,16,256]{2,1,0:T(8,128)(2,1)} %convert_element_type.425), calls=%async_computation.2 | async-start | bytes 131072 | tf_op jit(solution)/shard_map/all_to_all | solution.py:210
  307.2 14.9 %all-to-all-start.3 = ((bf16[128,2,256]{2,1,0:T(2,128)(2,1)}), bf16[128,2,256]{2,1,0:T(2,128)(2,1)S(1)}, u32[]{:S(2)}, u32[]{:S(2)}) async-start(bf16[128,2,256]{2,1,0:T(2,128)(2,1)} %reshape.531), calls=%async_computation.3 | async-start | bytes 262144 | tf_op jit(solution)/shard_map/all_to_all | solution.py:220
Sparse Core Ops, SparseCore 0:
  96.7 44.0 all-gather.1
where the time goes:
time: 346 us; the launch traced here: 339 us
  local copies, waits for them, and re-layouts  104 us (30%)
  other arithmetic  86.5 us (25%)
  waiting for transfers between devices  53.3 us (15%)
  blocking collectives  50.5 us (15%)
  starting transfers between devices  16 us (5%)
  between operations  15.4 us (4%)
  matrix products  13 us (4%)
    all_gather x1, waiting for transfers between devices, shards(): lax.all_gather(band_fields.astype(jnp.bfloat16), 'wide', axis=1, tiled=True)  39.6 us
    add x2, other arithmetic, upwind_flux(): jnp.maximum(face_speed, 0.0) * left_vals  38.3 us
    all_to_all x1, blocking collectives, shards(): lax.all_to_all(inverse_rows, ('wide', 'grp'), split_axis=1, concat_axis=2...  24.1 us
    broadcast_in_dim x1, other arithmetic, shards(): return (surface, new_states[:, None], tendency)  22 us
    unnamed x33, local copies, waits for them, and re-layouts  21.2 us
    all_gather x1, blocking collectives, shards(): lax.all_gather(coarse_flat.reshape(2, 1, TS * TS).astype(jnp.bfloat16), '...  17.1 us
    slice x2, local copies, waits for them, and re-layouts, upwind_flux(): speed_pad = jnp.pad(speeds, widths, mode='edge')  13.4 us
    dot_general x28, matrix products, contract(): return jnp.einsum(pattern, data, table, preferred_element_type=jnp.float32)  13 us
  transfers between devices with their start and end apart: 3, of which 3 were waited for; matrix products, arithmetic and copies ran while one was open for 2% of the time, Pallas kernels for 0%

commit v1 on v0

--- a/solution.py
+++ b/solution.py
@@ -10,6 +10,27 @@
 Z_TOP = 2.0
 DECAY_RATE = 0.5
 COURANT = 0.3
+
+
+def link_node(load):
+    k_now, block_now, tall = (lax.psum(1, "wide"), lax.axis_index("wide"), load.shape[1])
+    arrivals = [(jj, (jj + 1) % k_now) for jj in range(k_now)]
+    windows = [(jj, (jj - 1) % k_now) for jj in range(k_now)]
+    long_array = jnp.zeros((*load.shape[:1], k_now * tall, *load.shape[2:]), load.dtype)
+    long_array = lax.dynamic_update_slice_in_dim(long_array, load, block_now * tall, axis=1)
+    f_now = finding = load
+    u1 = k_now // 2
+    for t in range(1, u1 + 1):
+        f_now = lax.ppermute(f_now, "wide", arrivals)
+        long_array = lax.dynamic_update_slice_in_dim(
+            long_array, f_now, (block_now - t) % k_now * tall, axis=1
+        )
+        if t < k_now - u1:
+            finding = lax.ppermute(finding, "wide", windows)
+            long_array = lax.dynamic_update_slice_in_dim(
+                long_array, finding, (block_now + t) % k_now * tall, axis=1
+            )
+    return long_array
 
 
 def for_sending(shard):
@@ -173,9 +194,7 @@
     rank_index = jnp.sum(
         jnp.where(matches, jnp.arange(per_group, dtype=jnp.int32)[None, :], 0), axis=1
     )
-    column_strip = lax.all_gather(
-        band_fields.astype(jnp.bfloat16), "wide", axis=1, tiled=True
-    ).astype(band_fields.dtype)
+    column_strip = link_node(band_fields.astype(jnp.bfloat16)).astype(band_fields.dtype)
 
     def pick_strip(rank):
         return lax.dynamic_slice(

time: 346 us -> 362 us (1.046)
  starting transfers between devices: 16 us -> 72.6 us
  blocking collectives: 50.5 us -> 15.6 us
  between operations: 15.4 us -> 1.95 us
  waiting for transfers between devices: 53.3 us -> 59.7 us
    all_gather x1 -> x0, waiting for transfers between devices: 39.6 us -> none  [shards(): lax.all_gather(band_fields.astype(jnp.bfloat16), 'wide', axis=1, tiled=True)]
    ppermute x0 -> x15, waiting for transfers between devices: none -> 33.4 us  [the longest x8 19.5 us: link_node(): f_now = lax.ppermute(f_now, 'wide', arrivals)]
    all_to_all x2 -> x0, blocking collectives: 33.4 us -> none  [the longest x1 24.1 us: shards(): lax.all_to_all(inverse_rows, ('wide', 'grp'), split_axis=1, concat_axis=2...]
    ppermute x0 -> x15, starting transfers between devices: none -> 31.8 us  [the longest x7 30.4 us: link_node(): finding = lax.ppermute(finding, 'wide', windows)]
    all_to_all x0 -> x2, starting transfers between devices: none -> 15.9 us  [the longest x1 11.8 us: shards(): lax.all_to_all(inverse_rows, ('wide', 'grp'), split_axis=1, concat_axis=2...]
    all_to_all x0 -> x2, waiting for transfers between devices: none -> 12.5 us  [the longest x1 6.68 us: shards(): lax.all_to_all(inverse_rows, ('wide', 'grp'), split_axis=1, concat_axis=2...]
    all_to_all x1, starting transfers between devices: 11 us -> 18.2 us  [shards(): lax.all_to_all(for_sending(surface_band), 'grp', split_axis=0, concat_axi...]
    unnamed x33 -> x41, local copies, waits for them, and re-layouts: 21.2 us -> 22.6 us
  transfers between devices with their start and end apart: 3 -> 19, of which waited for: 3 -> 13; matrix products, arithmetic and copies ran while one was open for 2% -> 3% of each run, Pallas kernels for 0% -> 0%
where the time goes in v1:
time: 362 us; the launch traced here: 355 us
  local copies, waits for them, and re-layouts  106 us (29%)
  other arithmetic  86.5 us (24%)
  starting transfers between devices  72.6 us (20%)
  waiting for transfers between devices  59.7 us (16%)
  blocking collectives  15.6 us (4%)
  matrix products  12.9 us (4%)
    add x2, other arithmetic, upwind_flux(): jnp.maximum(face_speed, 0.0) * left_vals  38.2 us
    ppermute x7, starting transfers between devices, link_node(): finding = lax.ppermute(finding, 'wide', windows)  30.4 us
    unnamed x41, local copies, waits for them, and re-layouts  22.6 us
    broadcast_in_dim x1, other arithmetic, shards(): return (surface, new_states[:, None], tendency)  22.2 us
    ppermute x8, waiting for transfers between devices, link_node(): f_now = lax.ppermute(f_now, 'wide', arrivals)  19.5 us
    all_to_all x1, starting transfers between devices, shards(): lax.all_to_all(for_sending(surface_band), 'grp', split_axis=0, concat_axi...  18.2 us
    all_gather x1, blocking collectives, shards(): lax.all_gather(coarse_flat.reshape(2, 1, TS * TS).astype(jnp.bfloat16), '...  15.6 us
    ppermute x7, waiting for transfers between devices, link_node(): finding = lax.ppermute(finding, 'wide', windows)  13.9 us
  transfers between devices with their start and end apart: 19, of which 13 were waited for; matrix products, arithmetic and copies ran while one was open for 3% of the time, Pallas kernels for 0%

profile of v1, /device:TPU:1, one launch (start us, length us, event | category | flops | bytes accessed | tf_op | source)
XLA Modules:
  0.0 355.4 jit_solution(1812687824189227377)
XLA Ops:
  9.3 4.1 %copy.124 = bf16[6,2048,16]{2,0,1:T(8,128)(2,1)} copy(bf16[6,2048,16]{1,2,0:T(8,128)(2,1)S(1)} %maximum_bitcast_fusion) | data formatting | bytes 786432 | tf_op jit(solution)/shard_map/transpose | solution.py:168
  13.4 6.3 %reshape.527 = bf16[128,2,768]{2,1,0:T(2,128)(2,1)} reshape(bf16[2048,6,16]{2,1,0:T(8,128)(2,1)} %bitcast.240) | data formatting | bytes 786432
  19.7 11.8 %all-to-all-start = ((bf16[128,2,768]{2,1,0:T(2,128)(2,1)}), bf16[128,2,768]{2,1,0:T(2,128)(2,1)S(1)}, u32[]{:S(2)}, u32[]{:S(2)}) async-start(bf16[128,2,768]{2,1,0:T(2,128)(2,1)} %reshape.527), calls=%async_computation | async-start | bytes 786432 | tf_op jit(solution)/shard_map/all_to_all | solution.py:171
  37.0 6.7 %all-to-all-done = bf16[128,2,768]{2,1,0:T(2,128)(2,1)S(1)} async-done(((bf16[128,2,768]{2,1,0:T(2,128)(2,1)}), bf16[128,2,768]{2,1,0:T(2,128)(2,1)S(1)}, u32[]{:S(2)}, u32[]{:S(2)}) %all-to-all-start) | async-done | bytes 393248 | tf_op jit(solution)/shard_map/all_to_all | solution.py:171
  43.7 4.8 %reshape.528 = bf16[2048,6,16]{2,1,0:T(8,128)(2,1)} reshape(bf16[128,2,768]{2,1,0:T(2,128)(2,1)S(1)} %all-to-all-done) | data formatting | bytes 786432
  48.5 6.1 %copy.158 = bf16[6,128,16,16]{2,1,3,0:T(8,128)(2,1)S(1)} copy(bf16[6,128,16,16]{3,0,2,1:T(8,128)(2,1)} %bitcast.239) | data formatting | bytes 786432 | tf_op jit(solution)/shard_map/all_to_all | solution.py:171
  56.6 4.3 %copy.126 = bf16[3,16,128,16]{3,2,1,0:T(8,128)(2,1)S(1)} copy(bf16[3,16,128,16]{1,2,3,0:T(8,128)(2,1)} %get-tuple-element.58) | data formatting | bytes 393216 | tf_op jit(solution)/shard_map/slice | solution.py:172
  77.9 4.2 %all-to-all-start.1 = ((bf16[8,2,6144]{2,1,0:T(2,128)(2,1)}), bf16[8,2,6144]{2,1,0:T(2,128)(2,1)S(1)}, u32[]{:S(2)}, u32[]{:S(2)}) async-start(bf16[8,2,6144]{2,1,0:T(2,128)(2,1)} %reshape.529), calls=%async_computation.1 | async-start | bytes 393216 | tf_op jit(solution)/shard_map/all_to_all | solution.py:173
  82.2 5.8 %all-to-all-done.1 = bf16[8,2,6144]{2,1,0:T(2,128)(2,1)S(1)} async-done(((bf16[8,2,6144]{2,1,0:T(2,128)(2,1)}), bf16[8,2,6144]{2,1,0:T(2,128)(2,1)S(1)}, u32[]{:S(2)}, u32[]{:S(2)}) %all-to-all-start.1) | async-done | bytes 196640 | tf_op jit(solution)/shard_map/all_to_all | solution.py:173
  96.6 3.8 %collective-permute-start.3 = (bf16[3,128,256]{2,1,0:T(8,128)(2,1)}, bf16[3,128,256]{2,1,0:T(8,128)(2,1)S(1)}, u32[]{:S(2)}, u32[]{:S(2)}) collective-permute-start(bf16[3,128,256]{2,1,0:T(8,128)(2,1)} %collective-permute-done.1), channel_id=1, source_target_pairs={{0,120},{8,0},{16,8},{24,16},{32,24},{40,32},{48,40},{56,48},{64,5... | collective-permute-start | bytes 589832 | tf_op jit(solution)/shard_map/ppermute | solution.py:29
  103.3 5.1 %collective-permute-start.5 = (bf16[3,128,256]{2,1,0:T(8,128)(2,1)S(1)}, bf16[3,128,256]{2,1,0:T(8,128)(2,1)S(1)}, u32[]{:S(2)}, u32[]{:S(2)}) collective-permute-start(bf16[3,128,256]{2,1,0:T(8,128)(2,1)S(1)} %collective-permute-done.3), channel_id=1, source_target_pairs={{0,120},{8,0},{16,8},{24,16},{32,24},{40,32},{48,40},{56,48},{64,5... | collective-permute-start | bytes 589832 | tf_op jit(solution)/shard_map/ppermute | solution.py:29
  111.0 5.2 %collective-permute-start.7 = (bf16[3,128,256]{2,1,0:T(8,128)(2,1)S(1)}, bf16[3,128,256]{2,1,0:T(8,128)(2,1)S(1)}, u32[]{:S(2)}, u32[]{:S(2)}) collective-permute-start(bf16[3,128,256]{2,1,0:T(8,128)(2,1)S(1)} %collective-permute-done.5), channel_id=1, source_target_pairs={{0,120},{8,0},{16,8},{24,16},{32,24},{40,32},{48,40},{56,48},{64,5... | collective-permute-start | bytes 589832 | tf_op jit(solution)/shard_map/ppermute | solution.py:29
  118.9 5.2 %collective-permute-start.9 = (bf16[3,128,256]{2,1,0:T(8,128)(2,1)S(1)}, bf16[3,128,256]{2,1,0:T(8,128)(2,1)S(1)}, u32[]{:S(2)}, u32[]{:S(2)}) collective-permute-start(bf16[3,128,256]{2,1,0:T(8,128)(2,1)S(1)} %collective-permute-done.7), channel_id=1, source_target_pairs={{0,120},{8,0},{16,8},{24,16},{32,24},{40,32},{48,40},{56,48},{64,5... | collective-permute-start | bytes 589832 | tf_op jit(solution)/shard_map/ppermute | solution.py:29
  126.7 5.2 %collective-permute-start.11 = (bf16[3,128,256]{2,1,0:T(8,128)(2,1)S(1)}, bf16[3,128,256]{2,1,0:T(8,128)(2,1)S(1)}, u32[]{:S(2)}, u32[]{:S(2)}) collective-permute-start(bf16[3,128,256]{2,1,0:T(8,128)(2,1)S(1)} %collective-permute-done.9), channel_id=1, source_target_pairs={{0,120},{8,0},{16,8},{24,16},{32,24},{40,32},{48,40},{56,48},{64,5... | collective-permute-start | bytes 589832 | tf_op jit(solution)/shard_map/ppermute | solution.py:29
  134.6 5.2 %collective-permute-start.13 = (bf16[3,128,256]{2,1,0:T(8,128)(2,1)S(1)}, bf16[3,128,256]{2,1,0:T(8,128)(2,1)S(1)}, u32[]{:S(2)}, u32[]{:S(2)}) collective-permute-start(bf16[3,128,256]{2,1,0:T(8,128)(2,1)S(1)} %collective-permute-done.11), channel_id=1, source_target_pairs={{0,120},{8,0},{16,8},{24,16},{32,24},{40,32},{48,40},{56,48},{64,5... | collective-permute-start | bytes 589832 | tf_op jit(solution)/shard_map/ppermute | solution.py:29
  140.2 9.2 %collective-permute-done.12 = bf16[3,128,256]{2,1,0:T(8,128)(2,1)S(1)} collective-permute-done((bf16[3,128,256]{2,1,0:T(8,128)(2,1)S(1)}, bf16[3,128,256]{2,1,0:T(8,128)(2,1)S(1)}, u32[]{:S(2)}, u32[]{:S(2)}) %collective-permute-start.12) | collective-permute-done | bytes 196640 | tf_op jit(solution)/shard_map/ppermute | solution.py:24
  149.8 10.1 %collective-permute-done.14 = bf16[3,128,256]{2,1,0:T(8,128)(2,1)S(1)} collective-permute-done((bf16[3,128,256]{2,1,0:T(8,128)(2,1)S(1)}, bf16[3,128,256]{2,1,0:T(8,128)(2,1)S(1)}, u32[]{:S(2)}, u32[]{:S(2)}) %collective-permute-start.14) | collective-permute-done | bytes 196640 | tf_op jit(solution)/shard_map/ppermute | solution.py:24
  163.1 5.9 %while.1 = (s32[]{:T(128)}, f32[3,2048,256]{2,1,0:T(8,128)}, s32[2,3]{1,0:T(2,128)S(1)}, f32[2,3,64,64]{3,2,1,0:T(8,128)S(1)}, s32[]{:T(128)}) while((s32[]{:T(128)}, f32[3,2048,256]{2,1,0:T(8,128)}, s32[2,3]{1,0:T(2,128)S(1)}, f32[2,3,64,64]{3,2,1,0:T(8,128)S(1)}, s32[]{:T(128)}) %tuple.59), condition=%wide.while_cond, body=%wide.while_body.sunk | while | flops 2 | bytes 147581 | solution.py:200
  169.4 3.9 %fusion.8 = f32[2,64,128,128]{3,2,1,0:T(8,128)S(1)} fusion(bf16[2,1,64,128,128]{4,3,2,1,0:T(8,128)(2,1)} %param.7, f32[128,128]{1,0:T(8,128)S(1)} %get-tuple-element.81, f32[64]{0:T(128)S(1)} %copy-done.8, f32[2,128,128]{2,1,0:T(8,128)S(1)} %copy.134, f32[128,128]{1,0:T(8,128)S(1)} %get-tuple-element.80), kind=kLoop, calls=%fused_computation.22 | loop fusion | flops 16777216 | bytes 12845312 | tf_op jit(solution)/shard_map/vmap()/add | solution.py:76
  173.4 7.7 %fusion.246 = (f32[2,64,128,1]{3,2,1,0:T(8,128)}, f32[2,64,128,1]{3,2,1,0:T(8,128)}) fusion(f32[2,64,128,128]{3,2,1,0:T(8,128)S(1)} %fusion.8), kind=kLoop, calls=%fused_computation.369 | loop fusion | bytes 262144 | tf_op jit(solution)/shard_map/vmap(jit(_pad))/slice | solution.py:50
  182.3 5.4 %broadcast_multiply_fusion.1 = (f32[2,64,128,128]{3,2,1,0:T(8,128)}, f32[2,64,128,128]{3,2,1,0:T(8,128)S(1)}) fusion(f32[64]{0:T(128)S(1)} %multiply_exponential_fusion, f32[2,128,128]{2,1,0:T(8,128)S(1)} %copy.137, f32[2,128,128]{2,1,0:T(8,128)S(1)} %copy.139), kind=kLoop, calls=%fused_computation.25 | loop fusion | flops 4194304 | bytes 17039616 | tf_op jit(solution)/shard_map/vmap()/mul | solution.py:78
  191.1 13.4 %fusion.245 = (f32[2,64,128,1]{3,2,1,0:T(8,128)}, f32[2,64,128,1]{3,2,1,0:T(8,128)}) fusion(f32[2,64,128,128]{3,2,1,0:T(8,128)} %get-tuple-element.78), kind=kLoop, calls=%fused_computation.368 | loop fusion | bytes 262144 | tf_op jit(solution)/shard_map/vmap(jit(_pad))/slice | solution.py:51
  204.5 12.6 %fusion.3 = f32[2,64,129,128]{3,2,1,0:T(8,128)} fusion(f32[2,64,128,128]{3,2,1,0:T(8,128)S(1)} %bitcast.236, f32[2,64,1,128]{3,2,1,0:T(1,128)S(1)} %get-tuple-element.56, f32[2,64,1,128]{3,2,1,0:T(1,128)S(1)} %get-tuple-element.55, f32[2,64,1,128]{3,2,1,0:T(1,128)S(1)} %get-tuple-element.54, f32[2,64,128,128]{3,2,1,0:T(8,128)} %copy-done.1, ...), kind=kLoop, calls=%fused_computation.13 | loop fusion | flops 23248896 | bytes 25493504 | tf_op jit(solution)/shard_map/vmap()/add | solution.py:59
  217.1 25.6 %fusion.1 = f32[2,64,128,129]{3,2,1,0:T(8,128)} fusion(f32[2,64,128,128]{3,2,1,0:T(8,128)S(1)} %bitcast.236, f32[2,64,128,1]{3,2,1,0:T(8,128)} %get-tuple-element.52, f32[2,64,128,1]{3,2,1,0:T(8,128)} %get-tuple-element.51, f32[2,64,128,1]{3,2,1,0:T(8,128)} %get-tuple-element.50, f32[2,64,128,128]{3,2,1,0:T(8,128)} %get-tuple-element.78, ...), kind=kLoop, calls=%fused_computation.8 | loop fusion | flops 23248896 | bytes 25493504 | tf_op jit(solution)/shard_map/vmap()/add | solution.py:59
  242.7 22.2 %convert_bitcast_fusion = (bf16[2,1,64,128,128]{4,3,2,1,0:T(8,128)(2,1)}, f32[2,64,128,128]{3,2,1,0:T(8,128)}) fusion(f32[2,64,129,128]{3,2,1,0:T(8,128)} %fusion.3, f32[2,64,128,129]{3,2,1,0:T(8,128)} %fusion.1, bf16[2,1,64,128,128]{4,3,2,1,0:T(8,128)(2,1)} %param.7, f32[128,128]{1,0:T(8,128)S(1)} %get-tuple-element.81, f32[64]{0:T(128)S(1)} %copy-done.8, ...), kind=kLoop, calls=%fused_computation.23 | loop fusion | flops 31457280 | bytes 50594048 | tf_op jit(solution)/shard_map/broadcast_in_dim | solution.py:242
  268.7 9.8 %add.669 = f32[2,64,2,64,2]{4,3,2,1,0:T(8,128)} reshape(f32[2,128,128]{2,1,0:T(8,128)S(1)} %multiply_add_fusion) | data formatting | bytes 262144 | tf_op jit(solution)/shard_map/vmap()/add | solution.py:84
  278.5 4.6 %reduce_sum.30 = f32[2,64,64]{2,1,0:T(8,128)S(1)} reduce(f32[2,64,2,64,2]{4,3,2,1,0:T(8,128)} %add.669, f32[]{:T(128)} %constant.280.clone.1), dimensions={2,4}, to_apply=%region_2.3 | reduce | flops 24576 | bytes 163844 | tf_op jit(solution)/shard_map/vmap()/reduce_sum | solution.py:85
  283.2 15.6 %all_gather.3 = bf16[2,16,4096]{2,0,1:T(2,128)(2,1)S(1)} all-gather(bf16[2,1,4096]{2,0,1:T(2,128)(2,1)S(1)} %convert_element_type.422), channel_id=1, replica_groups=mesh['wide'=16,'grp'=8] {'wide'}, dimensions={1}, use_global_device_ids=true | all-gather | bytes 278528 | tf_op jit(solution)/shard_map/all_gather | solution.py:210
  300.7 18.2 %all-to-all-start.2 = ((bf16[8,16,256]{2,1,0:T(8,128)(2,1)}), bf16[8,16,256]{2,1,0:T(8,128)(2,1)S(1)}, u32[]{:S(2)}, u32[]{:S(2)}) async-start(bf16[8,16,256]{2,1,0:T(8,128)(2,1)} %convert_element_type.425), calls=%async_computation.2 | async-start | bytes 131072 | tf_op jit(solution)/shard_map/all_to_all | solution.py:229
  319.3 4.5 %all-to-all-done.2 = bf16[8,16,256]{2,1,0:T(8,128)(2,1)S(1)} async-done(((bf16[8,16,256]{2,1,0:T(8,128)(2,1)}), bf16[8,16,256]{2,1,0:T(8,128)(2,1)S(1)}, u32[]{:S(2)}, u32[]{:S(2)}) %all-to-all-start.2) | async-done | bytes 65568 | tf_op jit(solution)/shard_map/all_to_all | solution.py:229
  329.1 6.7 %all-to-all-start.3 = ((bf16[128,2,256]{2,1,0:T(2,128)(2,1)}), bf16[128,2,256]{2,1,0:T(2,128)(2,1)S(1)}, u32[]{:S(2)}, u32[]{:S(2)}) async-start(bf16[128,2,256]{2,1,0:T(2,128)(2,1)} %reshape.531), calls=%async_computation.3 | async-start | bytes 262144 | tf_op jit(solution)/shard_map/all_to_all | solution.py:239
  336.4 9.3 %all-to-all-done.3 = bf16[128,2,256]{2,1,0:T(2,128)(2,1)S(1)} async-done(((bf16[128,2,256]{2,1,0:T(2,128)(2,1)}), bf16[128,2,256]{2,1,0:T(2,128)(2,1)S(1)}, u32[]{:S(2)}, u32[]{:S(2)}) %all-to-all-start.3) | async-done | bytes 131104 | tf_op jit(solution)/shard_map/all_to_all | solution.py:239
  (212 shorter events, 90.9 us)
Async XLA Ops:
  6.4 25.1 %copy-start.12 = (s32[256]{0:T(256)S(1)}, s32[256]{0:T(256)}, u32[]{:S(2)}) copy-start(s32[256]{0:T(256)} %param.6) | copy-start | bytes 3076
  19.7 24.0 %all-to-all-start = ((bf16[128,2,768]{2,1,0:T(2,128)(2,1)}), bf16[128,2,768]{2,1,0:T(2,128)(2,1)S(1)}, u32[]{:S(2)}, u32[]{:S(2)}) async-start(bf16[128,2,768]{2,1,0:T(2,128)(2,1)} %reshape.527), calls=%async_computation | async-start | bytes 786432 | tf_op jit(solution)/shard_map/all_to_all | solution.py:171
  56.6 7.5 %copy-start.2 = (bf16[3,16,128,16]{1,2,3,0:T(8,128)(2,1)S(1)}, bf16[3,16,128,16]{1,2,3,0:T(8,128)(2,1)}, u32[]{:S(2)}) copy-start(bf16[3,16,128,16]{1,2,3,0:T(8,128)(2,1)} %get-tuple-element.57) | copy-start | bytes 589828
  64.1 6.9 %copy-start.4 = (f32[32,64]{1,0:T(8,128)S(1)}, f32[32,64]{1,0:T(8,128)}, u32[]{:S(2)}) copy-start(f32[32,64]{1,0:T(8,128)} %copy-done.3) | copy-start | bytes 24580
  67.3 14.8 %copy-start.9 = (f32[128]{0:T(128)S(1)}, f32[128]{0:T(128)}, u32[]{:S(2)}) copy-start(f32[128]{0:T(128)} %subtract_minimum_fusion) | copy-start | bytes 1540
  77.9 10.1 %all-to-all-start.1 = ((bf16[8,2,6144]{2,1,0:T(2,128)(2,1)}), bf16[8,2,6144]{2,1,0:T(2,128)(2,1)S(1)}, u32[]{:S(2)}, u32[]{:S(2)}) async-start(bf16[8,2,6144]{2,1,0:T(2,128)(2,1)} %reshape.529), calls=%async_computation.1 | async-start | bytes 393216 | tf_op jit(solution)/shard_map/all_to_all | solution.py:173
  90.9 5.6 %collective-permute-start.1 = (bf16[3,128,256]{2,1,0:T(8,128)(2,1)S(1)}, bf16[3,128,256]{2,1,0:T(8,128)(2,1)}, u32[]{:S(2)}, u32[]{:S(2)}) collective-permute-start(bf16[3,128,256]{2,1,0:T(8,128)(2,1)S(1)} %bitcast.247), channel_id=1, source_target_pairs={{0,120},{8,0},{16,8},{24,16},{32,24},{40,32},{48,40},{56,48},{64,5... | collective-permute-start | bytes 589832 | tf_op jit(solution)/shard_map/ppermute | solution.py:29
  91.5 8.9 %collective-permute-start = (bf16[3,128,256]{2,1,0:T(8,128)(2,1)S(1)}, bf16[3,128,256]{2,1,0:T(8,128)(2,1)}, u32[]{:S(2)}, u32[]{:S(2)}) collective-permute-start(bf16[3,128,256]{2,1,0:T(8,128)(2,1)S(1)} %bitcast.248), channel_id=1, source_target_pairs={{0,8},{8,16},{16,24},{24,32},{32,40},{40,48},{48,56},{56,64},{64,7... | collective-permute-start | bytes 589832 | tf_op jit(solution)/shard_map/ppermute | solution.py:24
  93.9 69.2 %copy-start.5 = (f32[2,3,64,64]{3,2,1,0:T(8,128)S(1)}, f32[2,3,64,64]{3,2,1,0:T(8,128)}, u32[]{:S(2)}) copy-start(f32[2,3,64,64]{3,2,1,0:T(8,128)} %custom-call.8) | copy-start | bytes 294916
  93.9 69.2 %copy-start.10 = (s32[2,3]{1,0:T(2,128)S(1)}, s32[2,3]{1,0:T(2,128)}, u32[]{:S(2)}) copy-start(s32[2,3]{1,0:T(2,128)} %copy.132) | copy-start | bytes 76
  96.6 6.7 %collective-permute-start.3 = (bf16[3,128,256]{2,1,0:T(8,128)(2,1)}, bf16[3,128,256]{2,1,0:T(8,128)(2,1)S(1)}, u32[]{:S(2)}, u32[]{:S(2)}) collective-permute-start(bf16[3,128,256]{2,1,0:T(8,128)(2,1)} %collective-permute-done.1), channel_id=1, source_target_pairs={{0,120},{8,0},{16,8},{24,16},{32,24},{40,32},{48,40},{56,48},{64,5... | collective-permute-start | bytes 589832 | tf_op jit(solution)/shard_map/ppermute | solution.py:29
  100.4 8.1 %collective-permute-start.2 = (bf16[3,128,256]{2,1,0:T(8,128)(2,1)}, bf16[3,128,256]{2,1,0:T(8,128)(2,1)S(1)}, u32[]{:S(2)}, u32[]{:S(2)}) collective-permute-start(bf16[3,128,256]{2,1,0:T(8,128)(2,1)} %collective-permute-done), channel_id=1, source_target_pairs={{0,8},{8,16},{16,24},{24,32},{32,40},{40,48},{48,56},{56,64},{64,7... | collective-permute-start | bytes 589832 | tf_op jit(solution)/shard_map/ppermute | solution.py:24
  103.3 7.7 %collective-permute-start.5 = (bf16[3,128,256]{2,1,0:T(8,128)(2,1)S(1)}, bf16[3,128,256]{2,1,0:T(8,128)(2,1)S(1)}, u32[]{:S(2)}, u32[]{:S(2)}) collective-permute-start(bf16[3,128,256]{2,1,0:T(8,128)(2,1)S(1)} %collective-permute-done.3), channel_id=1, source_target_pairs={{0,120},{8,0},{16,8},{24,16},{32,24},{40,32},{48,40},{56,48},{64,5... | collective-permute-start | bytes 589832 | tf_op jit(solution)/shard_map/ppermute | solution.py:29
  108.4 7.8 %collective-permute-start.4 = (bf16[3,128,256]{2,1,0:T(8,128)(2,1)S(1)}, bf16[3,128,256]{2,1,0:T(8,128)(2,1)S(1)}, u32[]{:S(2)}, u32[]{:S(2)}) collective-permute-start(bf16[3,128,256]{2,1,0:T(8,128)(2,1)S(1)} %collective-permute-done.2), channel_id=1, source_target_pairs={{0,8},{8,16},{16,24},{24,32},{32,40},{40,48},{48,56},{56,64},{64,7... | collective-permute-start | bytes 589832 | tf_op jit(solution)/shard_map/ppermute | solution.py:24
  108.5 60.9 %copy-start.8 = (f32[64]{0:T(128)S(1)}, f32[64]{0:T(128)}, u32[]{:S(2)}) copy-start(f32[64]{0:T(128)} %fusion.157) | copy-start | bytes 772
  111.0 7.8 %collective-permute-start.7 = (bf16[3,128,256]{2,1,0:T(8,128)(2,1)S(1)}, bf16[3,128,256]{2,1,0:T(8,128)(2,1)S(1)}, u32[]{:S(2)}, u32[]{:S(2)}) collective-permute-start(bf16[3,128,256]{2,1,0:T(8,128)(2,1)S(1)} %collective-permute-done.5), channel_id=1, source_target_pairs={{0,120},{8,0},{16,8},{24,16},{32,24},{40,32},{48,40},{56,48},{64,5... | collective-permute-start | bytes 589832 | tf_op jit(solution)/shard_map/ppermute | solution.py:29
  116.3 7.8 %collective-permute-start.6 = (bf16[3,128,256]{2,1,0:T(8,128)(2,1)S(1)}, bf16[3,128,256]{2,1,0:T(8,128)(2,1)S(1)}, u32[]{:S(2)}, u32[]{:S(2)}) collective-permute-start(bf16[3,128,256]{2,1,0:T(8,128)(2,1)S(1)} %collective-permute-done.4), channel_id=1, source_target_pairs={{0,8},{8,16},{16,24},{24,32},{32,40},{40,48},{48,56},{56,64},{64,7... | collective-permute-start | bytes 589832 | tf_op jit(solution)/shard_map/ppermute | solution.py:24
  118.9 7.8 %collective-permute-start.9 = (bf16[3,128,256]{2,1,0:T(8,128)(2,1)S(1)}, bf16[3,128,256]{2,1,0:T(8,128)(2,1)S(1)}, u32[]{:S(2)}, u32[]{:S(2)}) collective-permute-start(bf16[3,128,256]{2,1,0:T(8,128)(2,1)S(1)} %collective-permute-done.7), channel_id=1, source_target_pairs={{0,120},{8,0},{16,8},{24,16},{32,24},{40,32},{48,40},{56,48},{64,5... | collective-permute-start | bytes 589832 | tf_op jit(solution)/shard_map/ppermute | solution.py:29
  124.1 7.8 %collective-permute-start.8 = (bf16[3,128,256]{2,1,0:T(8,128)(2,1)S(1)}, bf16[3,128,256]{2,1,0:T(8,128)(2,1)S(1)}, u32[]{:S(2)}, u32[]{:S(2)}) collective-permute-start(bf16[3,128,256]{2,1,0:T(8,128)(2,1)S(1)} %collective-permute-done.6), channel_id=1, source_target_pairs={{0,8},{8,16},{16,24},{24,32},{32,40},{40,48},{48,56},{56,64},{64,7... | collective-permute-start | bytes 589832 | tf_op jit(solution)/shard_map/ppermute | solution.py:24
  126.7 7.9 %collective-permute-start.11 = (bf16[3,128,256]{2,1,0:T(8,128)(2,1)S(1)}, bf16[3,128,256]{2,1,0:T(8,128)(2,1)S(1)}, u32[]{:S(2)}, u32[]{:S(2)}) collective-permute-start(bf16[3,128,256]{2,1,0:T(8,128)(2,1)S(1)} %collective-permute-done.9), channel_id=1, source_target_pairs={{0,120},{8,0},{16,8},{24,16},{32,24},{40,32},{48,40},{56,48},{64,5... | collective-permute-start | bytes 589832 | tf_op jit(solution)/shard_map/ppermute | solution.py:29
  132.0 8.2 %collective-permute-start.10 = (bf16[3,128,256]{2,1,0:T(8,128)(2,1)S(1)}, bf16[3,128,256]{2,1,0:T(8,128)(2,1)S(1)}, u32[]{:S(2)}, u32[]{:S(2)}) collective-permute-start(bf16[3,128,256]{2,1,0:T(8,128)(2,1)S(1)} %collective-permute-done.8), channel_id=1, source_target_pairs={{0,8},{8,16},{16,24},{24,32},{32,40},{40,48},{48,56},{56,64},{64,7... | collective-permute-start | bytes 589832 | tf_op jit(solution)/shard_map/ppermute | solution.py:24
  134.6 15.2 %collective-permute-start.13 = (bf16[3,128,256]{2,1,0:T(8,128)(2,1)S(1)}, bf16[3,128,256]{2,1,0:T(8,128)(2,1)S(1)}, u32[]{:S(2)}, u32[]{:S(2)}) collective-permute-start(bf16[3,128,256]{2,1,0:T(8,128)(2,1)S(1)} %collective-permute-done.11), channel_id=1, source_target_pairs={{0,120},{8,0},{16,8},{24,16},{32,24},{40,32},{48,40},{56,48},{64,5... | collective-permute-start | bytes 589832 | tf_op jit(solution)/shard_map/ppermute | solution.py:29
  140.1 9.2 %collective-permute-start.12 = (bf16[3,128,256]{2,1,0:T(8,128)(2,1)S(1)}, bf16[3,128,256]{2,1,0:T(8,128)(2,1)S(1)}, u32[]{:S(2)}, u32[]{:S(2)}) collective-permute-start(bf16[3,128,256]{2,1,0:T(8,128)(2,1)S(1)} %collective-permute-done.10), channel_id=1, source_target_pairs={{0,8},{8,16},{16,24},{24,32},{32,40},{40,48},{48,56},{56,64},{64,7... | collective-permute-start | bytes 589832 | tf_op jit(solution)/shard_map/ppermute | solution.py:24
  149.4 10.5 %collective-permute-start.14 = (bf16[3,128,256]{2,1,0:T(8,128)(2,1)S(1)}, bf16[3,128,256]{2,1,0:T(8,128)(2,1)S(1)}, u32[]{:S(2)}, u32[]{:S(2)}) collective-permute-start(bf16[3,128,256]{2,1,0:T(8,128)(2,1)S(1)} %collective-permute-done.12), channel_id=1, source_target_pairs={{0,8},{8,16},{16,24},{24,32},{32,40},{40,48},{48,56},{56,64},{64,7... | collective-permute-start | bytes 589832 | tf_op jit(solution)/shard_map/ppermute | solution.py:24
  173.3 8.4 %copy-start = (f32[2,64,128,128]{3,2,1,0:T(8,128)}, f32[2,64,128,128]{3,2,1,0:T(8,128)S(1)}, u32[]{:S(2)}) copy-start(f32[2,64,128,128]{3,2,1,0:T(8,128)S(1)} %fusion.8) | copy-start | bytes 25165828
  182.3 22.2 %slice-start = ((s8[8388608]{0:T(1024)(128)(4,1)}), s8[4194304]{0:T(1024)(128)(4,1)S(1)}, s32[]{:S(2)}) async-start(s8[8388608]{0:T(1024)(128)(4,1)} %bitcast.235), calls=%async_computation.4 | async-start | bytes 8388608
  191.1 13.4 %slice-start.1 = ((s8[8388608]{0:T(1024)(128)(4,1)}), s8[4194304]{0:T(1024)(128)(4,1)S(1)}, s32[]{:S(2)}) async-start(s8[8388608]{0:T(1024)(128)(4,1)} %bitcast.235), calls=%async_computation.5 | async-start | bytes 8388608
  268.7 31.1 %copy-start.11 = (pred[2,4]{1,0:T(4,128)(4,1)S(1)}, pred[2,4]{1,0:T(4,128)(4,1)}, u32[]{:S(2)}) copy-start(pred[2,4]{1,0:T(4,128)(4,1)} %broadcast_in_dim.31) | copy-start | bytes 28
  278.5 45.8 %copy-start.6 = (f32[32,64]{1,0:T(8,128)S(1)}, f32[32,64]{1,0:T(8,128)}, u32[]{:S(2)}) copy-start(f32[32,64]{1,0:T(8,128)} %get-tuple-element.92) | copy-start | bytes 24580
  278.5 45.8 %copy-start.7 = (f32[32,64]{1,0:T(8,128)S(1)}, f32[32,64]{1,0:T(8,128)}, u32[]{:S(2)}) copy-start(f32[32,64]{1,0:T(8,128)} %get-tuple-element.93) | copy-start | bytes 24580
  300.7 23.1 %all-to-all-start.2 = ((bf16[8,16,256]{2,1,0:T(8,128)(2,1)}), bf16[8,16,256]{2,1,0:T(8,128)(2,1)S(1)}, u32[]{:S(2)}, u32[]{:S(2)}) async-start(bf16[8,16,256]{2,1,0:T(8,128)(2,1)} %convert_element_type.425), calls=%async_computation.2 | async-start | bytes 131072 | tf_op jit(solution)/shard_map/all_to_all | solution.py:229
  329.1 16.6 %all-to-all-start.3 = ((bf16[128,2,256]{2,1,0:T(2,128)(2,1)}), bf16[128,2,256]{2,1,0:T(2,128)(2,1)S(1)}, u32[]{:S(2)}, u32[]{:S(2)}) async-start(bf16[128,2,256]{2,1,0:T(2,128)(2,1)} %reshape.531), calls=%async_computation.3 | async-start | bytes 262144 | tf_op jit(solution)/shard_map/all_to_all | solution.py:239
  (2 other events, 9.7 us)
